TPU v7x, 512 devices: a whole 4x4x16 slice. The times are simulated.
512 devices in a mesh: view: 4 (over y_lo, core), wide: 128 (over y_hi, x, z).
Axes of the slice: x: 4, y: 4 (y_hi: 2, y_lo: 2; y = y_hi * 2 + y_lo), z: 16, core: 2. Of those that a mesh axis runs over, the one named last changes fastest.
Arguments:
- estimate: float32 [128, 512, 384], P('wide'), may hold values from 0.5 to 2
- observed: float32 [4, 128, 512, 384], P('view', None, 'wide'), may hold values from 0.25 to 4
- psf_x: float32 [4, 63], P('view'), may hold values from 0.01 to 1
- psf_y: float32 [4, 63], P('view'), may hold values from 0.01 to 1
- psf_z: float32 [4, 63], P('view'), may hold values from 0.01 to 1
Outputs:
- refined: float32 [128, 512, 384], P('wide')
All inputs are finite; a program needn't handle non-finite values.
Results may differ from a plain program's by a relative error of at most 0.0001.
Values sent between devices are 32-bit elements; how exact they have to be, the bound alone decides.
A program may use at most 64 MiB of HBM per device.

v0:
```python
import jax
import jax.numpy as jnp
from jax import lax
from jax.sharding import PartitionSpec as P

TAPS = 63
ITERS = 2


def band_matrix(tap_values, count):
    weights = tap_values / jnp.sum(tap_values)
    cell_index = jnp.arange(count, dtype=jnp.int32)
    offset = cell_index[:, None] - cell_index[None, :] + (TAPS - 1) // 2
    inside = (offset >= 0) & (offset < TAPS)
    picked = jnp.take(weights, jnp.clip(offset, 0, TAPS - 1))
    return jnp.where(inside, picked, jnp.zeros_like(picked))


def per_device(estimate, observed, psf_x, psf_y, psf_z):
    high = lax.Precision.HIGHEST
    depth_dev, x_cells, y_cells = estimate.shape
    z_cells = depth_dev * lax.axis_size("wide")
    view_count = lax.axis_size("view")
    kern_x = band_matrix(psf_x[0], x_cells)
    kern_y = band_matrix(psf_y[0], y_cells)
    kern_z = band_matrix(psf_z[0], z_cells)
    recorded = observed[0]
    current = estimate
    for iteration in range(ITERS):
        plane = jnp.einsum("zxy,wy->zxw", current, kern_y, precision=high)
        plane = jnp.einsum("vx,zxy->zvy", kern_x, plane, precision=high)
        pencil = lax.all_to_all(plane, "wide", split_axis=1, concat_axis=0, tiled=True)
        blurred = jnp.einsum("wz,zxy->wxy", kern_z, pencil, precision=high)
        quotient = recorded / blurred
        back_proj = jnp.einsum("zw,zxy->wxy", kern_z, quotient, precision=high)
        returned = lax.all_to_all(back_proj, "wide", split_axis=0, concat_axis=1, tiled=True)
        slab_back = jnp.einsum("xv,zxy->zvy", kern_x, returned, precision=high)
        correction = jnp.einsum("zxy,yw->zxw", slab_back, kern_y, precision=high)
        summed = lax.psum(correction, "view")
        current = current * summed / view_count
    return current


def solution(mesh):
    return jax.shard_map(
        per_device,
        mesh=mesh,
        in_specs=(
            P("wide", None, None),
            P("view", None, "wide", None),
            P("view", None),
            P("view", None),
            P("view", None),
        ),
        out_specs=P("wide", None, None),
        check_vma=False,
    )
```

profile of v0, /device:TPU:1, one launch (start us, length us, event | category | flops | bytes accessed | tf_op | source)
XLA Modules:
  0.0 541.2 jit_solution(16080332180041931032)
XLA Ops:
  16.8 40.8 %fusion.169 = f32[384,384]{1,0:T(8,128)S(1)} fusion(f32[]{:T(128)} %bitcast.118, f32[]{:T(128)} %bitcast.119, f32[]{:T(128)} %bitcast.120, f32[]{:T(128)} %bitcast.121, f32[]{:T(128)} %bitcast.122, f32[]{:T(128)} %bitcast.124, f32[]{:T(128)} %bitcast.123, f32[]{:T(128)} %bitcast.7, f32[]{:T(128)} %bitcast.9, f32[]{:T(128)} %bitcast.11, f32[]{:T(128)} %bitcast.13, ...), kind=kLoop, calls=%fused_computation.189 | loop fusion | flops 21233664 | bytes 590076 | tf_op jit(solution)/shard_map/jit(_where)/select_n | solution.py:16
  57.6 1.4 fusion.146
  59.0 41.0 %fusion.19 = f32[512,512]{1,0:T(8,128)S(1)} fusion(f32[]{:T(128)} %bitcast.239, f32[]{:T(128)} %bitcast.240, f32[]{:T(128)} %bitcast.241, f32[]{:T(128)} %bitcast.242, f32[]{:T(128)} %bitcast.243, f32[]{:T(128)} %bitcast.245, f32[]{:T(128)} %bitcast.244, f32[]{:T(128)} %bitcast.128, f32[]{:T(128)} %bitcast.130, f32[]{:T(128)} %bitcast.132, f32[]{:T(128)} %bitcast.134, ...), kind=kLoop, calls=%fused_computation.34 | loop fusion | flops 37748736 | bytes 1048828 | tf_op jit(solution)/shard_map/jit(_where)/select_n | solution.py:16
  100.0 1.4 convolution_bitcast_fusion.5
  101.5 1.7 copy.17
  103.2 23.1 %all-to-all-start = ((f32[1,512,384]{2,0,1:T(1,128)}), f32[1,512,384]{2,0,1:T(1,128)S(1)}, u32[]{:S(2)}, u32[]{:S(2)}) async-start(f32[1,512,384]{2,0,1:T(1,128)} %copy.17), calls=%async_computation | async-start | bytes 1572864 | tf_op jit(solution)/shard_map/all_to_all | solution.py:32
  128.0 97.2 %gather_fusion = f32[16384]{0:T(1024)S(1)} fusion(f32[63]{0:T(128)S(1)} %divide_bitcast_fusion, s32[16384]{0:T(1024)S(1)} %fusion.295), kind=kCustom, calls=%fused_computation | custom fusion | bytes 196608 | tf_op jit(solution)/shard_map/jit(_take)/gather | solution.py:15
  225.2 3.0 reduce.3
  229.5 2.0 convolution_divide_fusion.1
  232.8 57.0 %all_to_all.42 = f32[128,4,384]{2,1,0:T(4,128)S(1)} all-to-all(f32[128,4,384]{2,1,0:T(4,128)S(1)} %copy.20), channel_id=1, replica_groups=mesh['view'=4,'wide'=128] {'wide'}, dimensions={0} | all-to-all | bytes 1572864 | tf_op jit(solution)/shard_map/all_to_all | solution.py:36
  291.0 2.6 convolution_bitcast_fusion.4
  293.6 2.6 convolution_bitcast_fusion.1
  296.4 51.8 %all-reduce.3.cloned.1.call-done = f32[1,512,384]{2,1,0:T(8,128)} async-done(((f32[1,512,384]{2,1,0:T(8,128)}), f32[1,512,384]{2,1,0:T(8,128)}) %all-reduce.3.cloned.1.call-update) | async-done | bytes 786448 | tf_op jit(solution)/shard_map/psum | solution.py:39
  348.2 2.8 fusion.144
  351.0 2.7 convolution_bitcast_fusion.3
  353.6 1.7 copy.21
  355.4 58.6 %all_to_all.43 = f32[1,512,384]{2,0,1:T(1,128)S(1)} all-to-all(f32[1,512,384]{2,0,1:T(1,128)} %copy.21), channel_id=1, replica_groups=mesh['view'=4,'wide'=128] {'wide'}, dimensions={1} | all-to-all | bytes 1572864 | tf_op jit(solution)/shard_map/all_to_all | solution.py:32
  414.0 3.0 reduce.4
  418.3 2.0 convolution_divide_fusion
  421.7 51.8 %all_to_all.44 = f32[128,4,384]{2,1,0:T(4,128)S(1)} all-to-all(f32[128,4,384]{2,1,0:T(4,128)S(1)} %copy.24), channel_id=1, replica_groups=mesh['view'=4,'wide'=128] {'wide'}, dimensions={0} | all-to-all | bytes 1572864 | tf_op jit(solution)/shard_map/all_to_all | solution.py:36
  474.6 2.6 convolution_bitcast_fusion.2
  477.2 2.6 convolution_bitcast_fusion
  479.8 52.0 %all-reduce.5.cloned.1.call-done = f32[1,512,384]{2,1,0:T(8,128)} async-done(((f32[1,512,384]{2,1,0:T(8,128)}), f32[1,512,384]{2,1,0:T(8,128)}) %all-reduce.5.cloned.1.call-update) | async-done | bytes 786448 | tf_op jit(solution)/shard_map/psum | solution.py:39
  531.8 2.1 multiply_multiply_fusion
  (36 shorter events, 19.9 us)
Async XLA Ops:
  6.5 1.3 copy-start.2
  6.5 51.0 %copy-start = (f32[1,512,384]{2,1,0:T(8,128)S(1)}, f32[1,512,384]{2,1,0:T(8,128)}, u32[]{:S(2)}) copy-start(f32[1,512,384]{2,1,0:T(8,128)} %param.5) | copy-start | bytes 2359300
  103.2 23.3 %copy-start.3 = (f32[1,63]{1,0:T(1,128)S(1)}, f32[1,63]{1,0:T(1,128)}, u32[]{:S(2)}) copy-start(f32[1,63]{1,0:T(1,128)} %param.9) | copy-start | bytes 760
  103.2 122.0 %all-to-all-start = ((f32[1,512,384]{2,0,1:T(1,128)}), f32[1,512,384]{2,0,1:T(1,128)S(1)}, u32[]{:S(2)}, u32[]{:S(2)}) async-start(f32[1,512,384]{2,0,1:T(1,128)} %copy.17), calls=%async_computation | async-start | bytes 1572864 | tf_op jit(solution)/shard_map/all_to_all | solution.py:32
  126.3 221.9 %all-reduce.3.cloned.1.call-start = ((), (), s32[]{:S(2)}) async-start(), calls=%async_computation.4 | async-start | bytes 1572864 | tf_op jit(solution)/shard_map/psum | solution.py:39
  296.2 235.7 %all-reduce.5.cloned.1.call-start = ((), (), s32[]{:S(2)}) async-start(), calls=%async_computation.5 | async-start | bytes 1572864 | tf_op jit(solution)/shard_map/psum | solution.py:39
  479.7 52.1 %copy-start.1 = (f32[1,512,384]{2,1,0:T(8,128)S(1)}, f32[1,512,384]{2,1,0:T(8,128)}, u32[]{:S(2)}) copy-start(f32[1,512,384]{2,1,0:T(8,128)} %all-reduce.3.cloned.1.call-done) | copy-start | bytes 2359300
Sparse Core Ops, SparseCore 0:
  296.3 51.9 all-reduce.2
  479.9 51.8 all-reduce.4
where the time goes:
time: 550 us; the launch traced here: 541 us
  blocking collectives  167 us (30%)
  local copies, waits for them, and re-layouts  112 us (20%)
  waiting for transfers between devices  104 us (19%)
  other arithmetic  95.8 us (17%)
  matrix products  24.2 us (4%)
  starting transfers between devices  23.6 us (4%)
  between operations  14 us (3%)
    all_to_all x2, blocking collectives, per_device(): lax.all_to_all(back_proj, 'wide', split_axis=0, concat_axis=1, tiled=True)  109 us
    psum x2, waiting for transfers between devices, per_device(): summed = lax.psum(correction, 'view')  104 us
    gather x9, local copies, waits for them, and re-layouts, band_matrix(): picked = jnp.take(weights, jnp.clip(offset, 0, TAPS - 1))  103 us
    select_n x2, other arithmetic, band_matrix(): return jnp.where(inside, picked, jnp.zeros_like(picked))  81.8 us
    all_to_all x1, blocking collectives, per_device(): lax.all_to_all(plane, 'wide', split_axis=1, concat_axis=0, tiled=True)  58.6 us
    all_to_all x1, starting transfers between devices, per_device(): lax.all_to_all(plane, 'wide', split_axis=1, concat_axis=0, tiled=True)  23.1 us
  transfers between devices with their start and end apart: 3, of which 2 were waited for; matrix products, arithmetic and copies ran while one was open for 18% of the time, Pallas kernels for 0%

commit v1 on v0

v1 whole, which is shorter than its diff:
```python
import functools

import jax
import jax.numpy as jnp
from jax import lax
from jax.experimental import pallas as pl
from jax.experimental.pallas import tpu as pltpu
from jax.sharding import PartitionSpec as P

TAPS = 63
HALF = (TAPS - 1) // 2
ITERS = 2
MESH = pl.DeviceIdType.MESH
F32 = jnp.float32
BF16 = jnp.bfloat16

RING = 16
GROUPS = 8
Q = 4
PLANE = GROUPS * Q
J = 4
Y = 384
NZ = 128
ROWS = PLANE * Q * J


def iota(shape, axis):
    return lax.broadcasted_iota(jnp.int32, shape, axis)


def split(value):
    top = value.astype(BF16)
    return top, (value - top.astype(F32)).astype(BF16)


def dot(a, b):
    return jnp.dot(a, b, preferred_element_type=F32)


def dot3(a_top, a_low, b_top, b_low):
    return dot(a_top, b_top) + (dot(a_top, b_low) + dot(a_low, b_top))


def toeplitz(row, rows, width, first):
    full = width + 128
    wide = jnp.concatenate([row, jnp.zeros((1, full - 128), F32)], axis=1)
    spread = jnp.broadcast_to(wide, (rows, full))
    return pltpu.roll(spread, first % full, axis=1, stride=1, stride_axis=0)[:, :width]


def kernel(
    est, obs, psf, out,
    taps, mh, ml, mth, mtl, nh, nl, nth, ntl, kyh, kyl, kyth, kytl,
    u, s1, r1, s2, r2, back, rh, rl, wh, wl, blur, o1, o2, ob, slab,
    psf_s, psf_r, uin_s, uin_r, halo_s, halo_r, a1_s, a1_r, a2_s, a2_r, bk_s, bk_r,
    o1_s, o1_r, o2_s, o2_r, o3_s, o3_r, uo_s, uo_r, fw_s, fa_r, fb_r,
):
    q = lax.axis_index("view")
    w = lax.axis_index("wide")
    h = w // RING
    zc = w % RING
    p = h * Q + q

    def dev(hh, zz, qq):
        return {"view": qq, "wide": hh * RING + zz}

    def remote(src, dst, send, recv, where):
        return pltpu.make_async_remote_copy(
            src_ref=src, dst_ref=dst, send_sem=send, recv_sem=recv, device_id=where, device_id_type=MESH
        )

    def wait_for(ref, sem):
        pltpu.make_async_copy(ref, ref, sem).wait()

    def loop(low, high, body):
        lax.fori_loop(low, high, lambda i, c: (body(i), c)[1], 0)

    barrier = pltpu.get_barrier_semaphore()

    def greet_ring(d):
        pl.semaphore_signal(barrier, inc=1, device_id=dev(h, (zc + d) % RING, q), device_id_type=MESH)

    def greet_plane(d):
        other = (p + d) % PLANE
        pl.semaphore_signal(barrier, inc=1, device_id=dev(other // Q, zc, other % Q), device_id_type=MESH)

    loop(1, RING, greet_ring)
    loop(1, PLANE, greet_plane)
    pl.semaphore_wait(barrier, RING - 1 + PLANE - 1)

    def send_taps(d):
        remote(psf, taps.at[q], psf_s, psf_r, dev(h, zc, (q + d) % Q)).start()

    loop(1, Q, send_taps)
    pltpu.make_async_copy(psf, taps.at[q], psf_r).start()

    owner = zc % Q == q

    @pl.when(owner)
    def _():
        def send(d):
            t = (zc + d) % RING
            remote(est.at[pl.ds(t * 32, 32)], u.at[0, 1, pl.ds((zc // 4) * 32, 32)], uin_s, uin_r, dev(h, t, q)).start()

        loop(1, RING, send)
        pltpu.make_async_copy(est.at[pl.ds(zc * 32, 32)], u.at[0, 1, pl.ds((zc // 4) * 32, 32)], uin_r).start()

    def obs_first(d):
        c = (h + d) % GROUPS
        remote(obs.at[:, pl.ds(c * 16, 16)], o1.at[h], o1_s, o1_r.at[h], dev(c, zc, q)).start()

    loop(1, GROUPS, obs_first)
    pltpu.make_async_copy(obs.at[:, pl.ds(h * 16, 16)], o1.at[h], o1_r.at[h]).start()

    wait_for(taps, psf_r)

    norm = []
    for v in range(Q):
        raw = taps[v]
        norm.append(raw / jnp.sum(raw, axis=1, keepdims=True))

    def row_of(v, r):
        return norm[v][r : r + 1, :]

    low_ok = zc != 0
    high_ok = zc != RING - 1
    t_mat = jnp.concatenate([toeplitz(row_of(v, 3), 32, 128, 1) for v in range(Q)], axis=0)
    k_lane = iota((128, 128), 1)
    t_mat = jnp.where(((k_lane >= 32) | low_ok) & ((k_lane < 64) | high_ok), t_mat, 0.0)
    k_row = iota((128, 128), 0)
    tt_mat = jnp.zeros((128, 128), F32)
    for v in range(Q):
        block = toeplitz(row_of(v, 0), 128, 128, 32 * v - 63)
        tt_mat = jnp.where(k_lane // 32 == v, block, tt_mat)
    tt_mat = jnp.where(((k_row >= 32) | low_ok) & ((k_row < 64) | high_ok), tt_mat, 0.0)
    t_top, t_low = split(t_mat)
    tt_top, tt_low = split(tt_mat)
    r_row, r_lane = iota((ROWS, 128), 0), iota((ROWS, 128), 1)
    pick_rows = (((r_row // 16) + 32 * ((r_row // 4) % 4)) == r_lane).astype(F32).astype(BF16)
    c_row, c_lane = iota((128, Y), 0), iota((128, Y), 1)
    pick_cols = ((c_lane // 128) * 32 + c_lane % 32 == c_row).astype(F32).astype(BF16)
    same_j = (iota((ROWS, Y), 0) % 4) == ((iota((ROWS, Y), 1) // 32) % 4)
    for part, ref in ((t_top, mh), (t_low, ml)):
        rows = dot(pick_rows, part).astype(BF16)
        ref[...] = jnp.where(same_j, dot(rows, pick_cols), 0.0).astype(BF16)
    rt_row, rt_lane = iota((128, ROWS), 0), iota((128, ROWS), 1)
    pick_rows_t = (((rt_lane // 16) + 32 * ((rt_lane // 4) % 4)) == rt_row).astype(F32).astype(BF16)
    ct_row, ct_lane = iota((Y, 128), 0), iota((Y, 128), 1)
    pick_cols_t = ((ct_row // 128) * 32 + ct_row % 32 == ct_lane).astype(F32).astype(BF16)
    same_j_t = (iota((Y, ROWS), 1) % 4) == ((iota((Y, ROWS), 0) // 32) % 4)
    for part, ref in ((tt_top, mth), (tt_low, mtl)):
        rows = dot(pick_cols_t, part).astype(BF16)
        ref[...] = jnp.where(same_j_t, dot(rows, pick_rows_t), 0.0).astype(BF16)
    g_row, g_lane = iota((128, ROWS), 0), iota((128, ROWS), 1)
    g_pick = ((g_lane // 64) * 16 + (g_lane % 4) * 4 + (g_lane // 16) % 4) == g_row
    gt_row, gt_lane = iota((ROWS, 128), 0), iota((ROWS, 128), 1)
    gt_pick = ((gt_row // 64) * 16 + (gt_row % 4) * 4 + (gt_row // 16) % 4) == gt_lane
    for v in range(Q):
        chosen = (g_pick & ((g_lane // 4) % 4 == v)).astype(F32).astype(BF16)
        top, low = split(toeplitz(row_of(v, 5), NZ, NZ, -HALF))
        nh[v] = dot(top, chosen).astype(BF16)
        nl[v] = dot(low, chosen).astype(BF16)
        chosen = (gt_pick & ((gt_row // 4) % 4 == v)).astype(F32).astype(BF16)
        top, low = split(toeplitz(row_of(v, 2), NZ, NZ, -HALF))
        nth[:, v * NZ : (v + 1) * NZ] = dot(chosen, top).astype(BF16)
        ntl[:, v * NZ : (v + 1) * NZ] = dot(chosen, low).astype(BF16)
        top, low = split(toeplitz(row_of(v, 1), Y, Y, -HALF))
        kyth[v] = top
        kytl[v] = low
        top, low = split(toeplitz(row_of(v, 4), Y, Y, -HALF))
        kyh[v] = top
        kyl[v] = low

    def send_plane(send_buf, recv_buf, send, recv, chunk):
        def one(k):
            other = chunk * 8 + k

            @pl.when(other != p)
            def _():
                remote(send_buf.at[other], recv_buf.at[p], send, recv, dev(other // Q, zc, other % Q)).start()

            @pl.when(other == p)
            def _():
                pltpu.make_async_copy(send_buf.at[other], recv_buf.at[p], recv).start()

        loop(0, 8, one)

    left = (zc + RING - 1) % RING
    right = (zc + 1) % RING

    for it in range(ITERS):
        if it == 0:
            wait_for(u.at[0, 1], uin_r)
        remote(u.at[it, 1], u.at[it, 2], halo_s.at[it, 0], halo_r.at[it, 0], dev(h, left, q)).start()
        remote(u.at[it, 1], u.at[it, 0], halo_s.at[it, 1], halo_r.at[it, 1], dev(h, right, q)).start()

        if it == 0:
            a = zc // 8
            b = zc % 8

            def obs_second(d):
                hs = (h + d) % GROUPS
                t = 2 * hs + a
                wait_for(o1.at[hs], o1_r.at[hs])

                @pl.when(t != zc)
                def _():
                    remote(o1.at[hs], o2.at[b], o2_s, o2_r.at[b], dev(h, t, q)).start()

                @pl.when(t == zc)
                def _():
                    pltpu.make_async_copy(o1.at[hs], o2.at[b], o2_r.at[b]).start()

            loop(0, GROUPS, obs_second)

        wait_for(u.at[it, 2], halo_r.at[it, 0])
        wait_for(u.at[it, 0], halo_r.at[it, 1])

        u_top, u_low = split(u[it].reshape(3 * NZ, Y))
        rh[0 : 3 * NZ] = u_top
        rl[0 : 3 * NZ] = u_low

        def forward(c):
            at = pl.ds(pl.multiple_of(c * 128, 128), 128)
            got = dot3(mh[at], ml[at], rh[0 : 3 * NZ], rl[0 : 3 * NZ])
            s1[it, pl.ds(c * 8, 8)] = got.reshape(8, 16, Y)
            send_plane(s1.at[it], r1.at[it], a1_s.at[it], a1_r.at[it], c)

        loop(0, 4, forward)
        wait_for(r1.at[it], a1_r.at[it])

        r_top, r_low = split(r1[it].reshape(ROWS, Y))
        rh[...] = r_top
        rl[...] = r_low

        def blur_view(v):
            z_top, z_low = split(dot3(nh[v], nl[v], rh[...], rl[...]))
            blur[v] = dot3(z_top, z_low, kyth[v], kytl[v])

        loop(0, Q, blur_view)

        if it == 0:
            def obs_third(b):
                wait_for(o2.at[b], o2_r.at[b])

                def one(i):
                    mine = (b == h) & (i == q)
                    dst = ob.at[q, pl.ds(h * 16, 16)]

                    @pl.when(jnp.logical_not(mine))
                    def _():
                        remote(o2.at[b, i], dst, o3_s, o3_r, dev(b, zc, i)).start()

                    @pl.when(mine)
                    def _():
                        pltpu.make_async_copy(o2.at[b, i], dst, o3_r).start()

                loop(0, Q, one)

            loop(0, GROUPS, obs_third)
            wait_for(ob, o3_r)

        def back_view(v):
            q_top, q_low = split(ob[v] / blur[v])
            w_top, w_low = split(dot3(q_top, q_low, kyh[v], kyl[v]))
            wh[pl.ds(pl.multiple_of(v * NZ, NZ), NZ)] = w_top
            wl[pl.ds(pl.multiple_of(v * NZ, NZ), NZ)] = w_low

        loop(0, Q, back_view)

        def backward(c):
            at = pl.ds(pl.multiple_of(c * 128, 128), 128)
            got = dot3(nth[at], ntl[at], wh[...], wl[...])
            s2[it, pl.ds(c * 8, 8)] = got.reshape(8, 16, Y)
            send_plane(s2.at[it], r2.at[it], a2_s.at[it], a2_r.at[it], c)

        loop(0, 4, backward)
        wait_for(r2.at[it], a2_r.at[it])

        r_top, r_low = split(r2[it].reshape(ROWS, Y))
        rh[...] = r_top
        rl[...] = r_low

        def piece(k):
            return dot3(mth[k * NZ : (k + 1) * NZ], mtl[k * NZ : (k + 1) * NZ], rh[...], rl[...])

        back[it, 0] = piece(0)
        remote(back.at[it, 0], back.at[it, 4], bk_s.at[it, 0], bk_r.at[it, 0], dev(h, left, q)).start()
        back[it, 2] = piece(2)
        remote(back.at[it, 2], back.at[it, 3], bk_s.at[it, 1], bk_r.at[it, 1], dev(h, right, q)).start()
        mine = piece(1)
        wait_for(back.at[it, 4], bk_r.at[it, 0])
        wait_for(back.at[it, 3], bk_r.at[it, 1])
        u[it + 1, 1] = u[it, 1] * (mine + back[it, 3] + back[it, 4]) * (1.0 / Q)

    def send_out(j):
        t = 4 * j + q
        src = u.at[ITERS, 1, pl.ds(j * 32, 32)]
        dst = slab.at[pl.ds(zc * 32, 32)]

        @pl.when(t != zc)
        def _():
            remote(src, dst, uo_s, uo_r.at[zc], dev(h, t, q)).start()

        @pl.when(t == zc)
        def _():
            pltpu.make_async_copy(src, dst, uo_r.at[zc]).start()

    loop(0, J, send_out)
    home = zc % Q
    role = q ^ home

    @pl.when(role == 0)
    def _():
        def forward_out(d):
            t = (zc + d) % RING
            at = pl.ds(t * 32, 32)
            wait_for(slab.at[at], uo_r.at[t])
            remote(slab.at[at], slab.at[at], fw_s.at[0], fa_r.at[t], dev(h, zc, q ^ 2)).start()
            remote(slab.at[at], slab.at[at], fw_s.at[1], fb_r.at[t], dev(h, zc, q ^ 1)).start()

        loop(0, RING, forward_out)
        wait_for(slab, fw_s.at[0])
        wait_for(slab, fw_s.at[1])

    @pl.when(role == 2)
    def _():
        def forward_again(d):
            t = (zc + d) % RING
            at = pl.ds(t * 32, 32)
            wait_for(slab.at[at], fa_r.at[t])
            remote(slab.at[at], slab.at[at], fw_s.at[1], fb_r.at[t], dev(h, zc, q ^ 1)).start()

        loop(0, RING, forward_again)
        wait_for(slab, fw_s.at[1])

    @pl.when((role == 1) | (role == 3))
    def _():
        def last(t):
            wait_for(slab.at[pl.ds(t * 32, 32)], fb_r.at[t])

        loop(0, RING, last)

    out[0] = slab[...]

    @pl.when(owner)
    def _():
        wait_for(est.at[pl.ds(0, 480)], uin_s)

    def wait_bytes(count, ref, sem):
        loop(0, count, lambda i: wait_for(ref, sem))

    wait_bytes(Q - 1, psf, psf_s)
    wait_for(o1.at[pl.ds(0, GROUPS - 1)], o1_s)
    kept2 = (zc % 2 == zc // 8).astype(jnp.int32)
    wait_bytes(GROUPS - kept2, o1.at[0], o2_s)
    wait_for(s1.at[0, pl.ds(0, PLANE - 1)], o3_s)
    for it in range(ITERS):
        for k in range(2):
            wait_for(u.at[it, 1], halo_s.at[it, k])
            wait_for(back.at[it, 0], bk_s.at[it, k])
        wait_for(s1.at[it, pl.ds(0, PLANE - 1)], a1_s.at[it])
        wait_for(s2.at[it, pl.ds(0, PLANE - 1)], a2_s.at[it])
    kept = (zc % Q == q).astype(jnp.int32)
    wait_bytes(J - kept, slab.at[pl.ds(0, 32)], uo_s)


def per_device(estimate, observed, psf_x, psf_y, psf_z):
    rows = jnp.concatenate([psf_x, psf_y, psf_z], axis=0)
    rows = jnp.concatenate([rows, jnp.flip(rows, axis=1)], axis=0)
    psf = jnp.pad(rows, ((0, 2), (0, 128 - TAPS)))
    recorded = jnp.transpose(observed[0], (1, 0, 2))
    vmem = pl.BlockSpec(memory_space=pltpu.VMEM)
    sem = pltpu.SemaphoreType.DMA
    return pl.pallas_call(
        kernel,
        out_shape=jax.ShapeDtypeStruct((1, 512, Y), F32),
        in_specs=[vmem] * 3,
        out_specs=vmem,
        scratch_shapes=[
            pltpu.VMEM((Q, 8, 128), F32),
            pltpu.VMEM((ROWS, Y), BF16),
            pltpu.VMEM((ROWS, Y), BF16),
            pltpu.VMEM((Y, ROWS), BF16),
            pltpu.VMEM((Y, ROWS), BF16),
            pltpu.VMEM((Q, NZ, ROWS), BF16),
            pltpu.VMEM((Q, NZ, ROWS), BF16),
            pltpu.VMEM((ROWS, Q * NZ), BF16),
            pltpu.VMEM((ROWS, Q * NZ), BF16),
            pltpu.VMEM((Q, Y, Y), BF16),
            pltpu.VMEM((Q, Y, Y), BF16),
            pltpu.VMEM((Q, Y, Y), BF16),
            pltpu.VMEM((Q, Y, Y), BF16),
            pltpu.VMEM((ITERS + 1, 3, NZ, Y), F32),
            pltpu.VMEM((ITERS, PLANE, 16, Y), F32),
            pltpu.VMEM((ITERS, PLANE, 16, Y), F32),
            pltpu.VMEM((ITERS, PLANE, 16, Y), F32),
            pltpu.VMEM((ITERS, PLANE, 16, Y), F32),
            pltpu.VMEM((ITERS, 5, NZ, Y), F32),
            pltpu.VMEM((ROWS, Y), BF16),
            pltpu.VMEM((ROWS, Y), BF16),
            pltpu.VMEM((ROWS, Y), BF16),
            pltpu.VMEM((ROWS, Y), BF16),
            pltpu.VMEM((Q, NZ, Y), F32),
            pltpu.VMEM((GROUPS, 4, 16, Y), F32),
            pltpu.VMEM((GROUPS, 4, 16, Y), F32),
            pltpu.VMEM((Q, NZ, Y), F32),
            pltpu.VMEM((512, Y), F32),
            sem, sem,
            sem, sem,
            sem((ITERS, 2)), sem((ITERS, 2)),
            sem((ITERS,)), sem((ITERS,)),
            sem((ITERS,)), sem((ITERS,)),
            sem((ITERS, 2)), sem((ITERS, 2)),
            sem, sem((GROUPS,)),
            sem, sem((GROUPS,)),
            sem, sem,
            sem, sem((RING,)),
            sem((2,)), sem((RING,)), sem((RING,)),
        ],
        compiler_params=pltpu.CompilerParams(
            collective_id=0, has_side_effects=True, vmem_limit_bytes=48 * 1024 * 1024
        ),
    )(estimate[0], recorded, psf)


def solution(mesh):
    return jax.shard_map(
        per_device,
        mesh=mesh,
        in_specs=(
            P("wide", None, None),
            P("view", None, "wide", None),
            P("view", None),
            P("view", None),
            P("view", None),
        ),
        out_specs=P("wide", None, None),
        check_vma=False,
    )
```

time: 550 us -> 182 us (0.33)
  the two profiles are of different devices: /device:TPU:1 before, /device:TPU:15 now
where the time goes in v1:
time: 182 us
  Pallas kernels  179 us (98%)
  local copies, waits for them, and re-layouts  3.02 us (2%)
    pallas_call x1, Pallas kernels, per_device(): pl.pallas_call(kernel, out_shape=jax.ShapeDtypeStruct((1, 512, Y), F32),...  179 us

profile of v1, /device:TPU:15, one launch (start us, length us, event | category | flops | bytes accessed | tf_op | source)
XLA Modules:
  0.0 181.9 jit_solution(9228835625655538536)
XLA Ops:
  0.0 0.0 copy-start.1
  0.0 0.0 copy-start.2
  0.0 0.0 copy-start.3
  0.0 0.6 copy-done.1
  0.7 0.0 copy-done.2
  0.7 0.0 copy-done.3
  0.7 0.1 rev.4
  0.8 0.0 copy-start
  0.8 1.3 copy.8
  2.1 0.1 copy-done
  2.2 178.8 %shard_map.55 = f32[1,512,384]{2,1,0:T(8,128)S(1)} custom-call(f32[512,384]{1,0:T(8,128)S(1)} %bitcast.7, f32[4,128,384]{2,1,0:T(8,128)S(1)} %bitcast.6, f32[8,128]{1,0:T(8,128)S(1)} %select_maximum_fusion.psf), custom_call_target="tpu_custom_call" | custom-call | tf_op jit(solution)/shard_map/pallas_call | solution.py:375
  181.0 0.9 copy.10
  (2 shorter events, 0.0 us)
Async XLA Ops:
  0.0 0.7 copy-start.1
  0.0 0.7 copy-start.2
  0.0 0.7 copy-start.3
  0.8 1.4 copy-start

commit v2 on v0

v2 whole, which is shorter than its diff:
```python
import functools

import jax
import jax.numpy as jnp
from jax import lax
from jax.experimental import pallas as pl
from jax.experimental.pallas import tpu as pltpu
from jax.sharding import PartitionSpec as P

TAPS = 63
HALF = (TAPS - 1) // 2
ITERS = 2
MESH = pl.DeviceIdType.MESH
F32 = jnp.float32
BF16 = jnp.bfloat16

RING = 16
GROUPS = 8
Q = 4
PLANE = GROUPS * Q
J = 4
Y = 384
NZ = 128
LANES = 128
CHUNKS = Y // LANES
ROWS = PLANE * Q * J


def iota(shape, axis):
    return lax.broadcasted_iota(jnp.int32, shape, axis)


def split(value):
    top = value.astype(BF16)
    return top, (value - top.astype(F32)).astype(BF16)


def dot(a, b):
    return jnp.dot(a, b, preferred_element_type=F32)


def dot3(a_top, a_low, b_top, b_low):
    return dot(a_top, b_top) + (dot(a_top, b_low) + dot(a_low, b_top))


def toeplitz(row, rows, width, first):
    full = width + 128
    wide = jnp.concatenate([row, jnp.zeros((1, full - 128), F32)], axis=1)
    spread = jnp.broadcast_to(wide, (rows, full))
    return pltpu.roll(spread, first % full, axis=1, stride=1, stride_axis=0)[:, :width]


def kernel(
    est, obs, psf, out,
    taps, mh, ml, mth, mtl, nh, nl, nth, ntl, kyh, kyl, kyth, kytl,
    u, s1, r1, s2, r2, back, xb, zb, ztop, zlow, wb, o1, o2, ob,
    psf_s, psf_r, uin_s, uin_r, halo_s, halo_r, a1_s, a1_r, a2_s, a2_r, bk_s, bk_r,
    o1_s, o1_r, o2_s, o2_r, o3_s, o3_r, uo_s, uo_r, fw_s, fa_r, fb_r,
):
    q = lax.axis_index("view")
    w = lax.axis_index("wide")
    h = w // RING
    zc = w % RING
    p = h * Q + q

    def dev(hh, zz, qq):
        return {"view": qq, "wide": hh * RING + zz}

    def remote(src, dst, send, recv, where):
        return pltpu.make_async_remote_copy(
            src_ref=src, dst_ref=dst, send_sem=send, recv_sem=recv, device_id=where, device_id_type=MESH
        )

    def wait_for(ref, sem):
        pltpu.make_async_copy(ref, ref, sem).wait()

    def loop(low, high, body):
        lax.fori_loop(low, high, lambda i, c: (body(i), c)[1], 0)

    barrier = pltpu.get_barrier_semaphore()

    def greet_ring(d):
        pl.semaphore_signal(barrier, inc=1, device_id=dev(h, (zc + d) % RING, q), device_id_type=MESH)

    def greet_plane(d):
        other = (p + d) % PLANE
        pl.semaphore_signal(barrier, inc=1, device_id=dev(other // Q, zc, other % Q), device_id_type=MESH)

    loop(1, RING, greet_ring)
    loop(1, PLANE, greet_plane)
    pl.semaphore_wait(barrier, RING - 1 + PLANE - 1)

    def wait_bytes(count, ref, sem):
        loop(0, count, lambda i: wait_for(ref, sem))

    drains = []
    owner = zc % Q == q
    left = (zc + RING - 1) % RING
    right = (zc + 1) % RING

    def partner(k):
        step = k // 2
        x = (h + step) % 4
        y = (h // 4 * 2 + q // 2 + step // 4 + step) % 4
        return (y // 2 * 4 + x) * Q + y % 2 * 2 + (q + k) % 2

    def send_plane(send_buf, recv_buf, send, recv, first, count):
        def one(i):
            k = first + i
            other = partner(k)

            @pl.when(k != 0)
            def _():
                remote(send_buf.at[k], recv_buf.at[p], send, recv, dev(other // Q, zc, other % Q)).start()

            @pl.when(k == 0)
            def _():
                pltpu.make_async_copy(send_buf.at[k], recv_buf.at[p], recv).start()

        loop(0, count, one)

    def lanes(c):
        return pl.ds(c * LANES, LANES)

    def pair(ref, value):
        top, low = split(value)
        ref[:, 0:LANES] = top
        ref[:, LANES:] = low

    def times_pair(a_top, a_low, ref):
        got = dot(a_top, ref[...])
        return got[:, 0:LANES] + (got[:, LANES:] + dot(a_low, ref[:, 0:LANES]))

    def taps_out():
        def send_taps(d):
            remote(psf, taps.at[q], psf_s, psf_r, dev(h, zc, (q + d) % Q)).start()

        loop(1, Q, send_taps)
        pltpu.make_async_copy(psf, taps.at[q], psf_r).start()
        drains.append(lambda: wait_bytes(Q - 1, psf, psf_s))

    def estimate_in():
        @pl.when(owner)
        def _():
            for c in range(CHUNKS):
                mine = u.at[0, c, 1, pl.ds((zc // 4) * 32, 32)]

                def send(i):
                    t = (zc + 8 + (1 - 2 * (i % 2)) * (i // 2)) % RING
                    remote(est.at[pl.ds(t * 32, 32), lanes(c)], mine, uin_s, uin_r.at[c], dev(h, t, q)).start()

                loop(1, RING, send)
                pltpu.make_async_copy(est.at[pl.ds(zc * 32, 32), lanes(c)], mine, uin_r.at[c]).start()

        def drain():
            @pl.when(owner)
            def _():
                wait_for(est.at[pl.ds(0, 480)], uin_s)

        drains.append(drain)

    def estimate_wait(c):
        wait_for(u.at[0, c, 1], uin_r.at[c])

    def observed_first():
        def obs_first(d):
            c = (h + d) % GROUPS
            remote(obs.at[:, pl.ds(c * 16, 16)], o1.at[h], o1_s, o1_r.at[h], dev(c, zc, q)).start()

        loop(1, GROUPS, obs_first)
        pltpu.make_async_copy(obs.at[:, pl.ds(h * 16, 16)], o1.at[h], o1_r.at[h]).start()
        drains.append(lambda: wait_for(o1.at[pl.ds(0, GROUPS - 1)], o1_s))

    def matrices():
        wait_for(taps, psf_r)

        norm = []
        for v in range(Q):
            raw = taps[v]
            norm.append(raw / jnp.sum(raw, axis=1, keepdims=True))

        def row_of(v, r):
            return norm[v][r : r + 1, :]

        low_ok = zc != 0
        high_ok = zc != RING - 1
        t_mat = jnp.concatenate([toeplitz(row_of(v, 3), 32, 128, 1) for v in range(Q)], axis=0)
        k_lane = iota((128, 128), 1)
        t_mat = jnp.where(((k_lane >= 32) | low_ok) & ((k_lane < 64) | high_ok), t_mat, 0.0)
        k_row = iota((128, 128), 0)
        tt_mat = jnp.zeros((128, 128), F32)
        for v in range(Q):
            block = toeplitz(row_of(v, 0), 128, 128, 32 * v - 63)
            tt_mat = jnp.where(k_lane // 32 == v, block, tt_mat)
        tt_mat = jnp.where(((k_row >= 32) | low_ok) & ((k_row < 64) | high_ok), tt_mat, 0.0)
        t_top, t_low = split(t_mat)
        tt_top, tt_low = split(tt_mat)
        r_row, r_lane = iota((ROWS, 128), 0), iota((ROWS, 128), 1)
        pick_rows = ((partner(r_row // 16) + 32 * ((r_row // 4) % 4)) == r_lane).astype(F32).astype(BF16)
        c_row, c_lane = iota((128, Y), 0), iota((128, Y), 1)
        pick_cols = ((c_lane // 128) * 32 + c_lane % 32 == c_row).astype(F32).astype(BF16)
        same_j = (iota((ROWS, Y), 0) % 4) == ((iota((ROWS, Y), 1) // 32) % 4)
        for part, ref in ((t_top, mh), (t_low, ml)):
            rows = dot(pick_rows, part).astype(BF16)
            ref[...] = jnp.where(same_j, dot(rows, pick_cols), 0.0).astype(BF16)
        rt_row, rt_lane = iota((128, ROWS), 0), iota((128, ROWS), 1)
        pick_rows_t = (((rt_lane // 16) + 32 * ((rt_lane // 4) % 4)) == rt_row).astype(F32).astype(BF16)
        ct_row, ct_lane = iota((Y, 128), 0), iota((Y, 128), 1)
        pick_cols_t = ((ct_row // 128) * 32 + ct_row % 32 == ct_lane).astype(F32).astype(BF16)
        same_j_t = (iota((Y, ROWS), 1) % 4) == ((iota((Y, ROWS), 0) // 32) % 4)
        for part, ref in ((tt_top, mth), (tt_low, mtl)):
            rows = dot(pick_cols_t, part).astype(BF16)
            ref[...] = jnp.where(same_j_t, dot(rows, pick_rows_t), 0.0).astype(BF16)
        g_row, g_lane = iota((128, ROWS), 0), iota((128, ROWS), 1)
        g_pick = ((g_lane // 64) * 16 + (g_lane % 4) * 4 + (g_lane // 16) % 4) == g_row
        gt_row, gt_lane = iota((ROWS, 128), 0), iota((ROWS, 128), 1)
        gt_p = partner(gt_row // 16)
        gt_pick = ((gt_p // 4) * 16 + (gt_row % 4) * 4 + gt_p % 4) == gt_lane
        for v in range(Q):
            chosen = (g_pick & ((g_lane // 4) % 4 == v)).astype(F32).astype(BF16)
            top, low = split(toeplitz(row_of(v, 5), NZ, NZ, -HALF))
            nh[v] = dot(top, chosen).astype(BF16)
            nl[v] = dot(low, chosen).astype(BF16)
            chosen = (gt_pick & ((gt_row // 4) % 4 == v)).astype(F32).astype(BF16)
            top, low = split(toeplitz(row_of(v, 2), NZ, NZ, -HALF))
            nth[:, v * NZ : (v + 1) * NZ] = dot(chosen, top).astype(BF16)
            ntl[:, v * NZ : (v + 1) * NZ] = dot(chosen, low).astype(BF16)
            top, low = split(toeplitz(row_of(v, 1), Y, Y, -HALF))
            kyth[v] = top
            kytl[v] = low
            top, low = split(toeplitz(row_of(v, 4), Y, Y, -HALF))
            kyh[v] = top
            kyl[v] = low

    def halo(it, c):
        own = u.at[it, c, 1]
        remote(own, u.at[it, c, 2], halo_s.at[it, c, 0], halo_r.at[it, c, 0], dev(h, left, q)).start()
        remote(own, u.at[it, c, 0], halo_s.at[it, c, 1], halo_r.at[it, c, 1], dev(h, right, q)).start()
        drains.append(lambda: [wait_for(own, halo_s.at[it, c, k]) for k in range(2)])

    def halo_wait(it, c):
        wait_for(u.at[it, c, 2], halo_r.at[it, c, 0])
        wait_for(u.at[it, c, 0], halo_r.at[it, c, 1])

    def observed_second():
        a = zc // 8
        b = zc % 8

        def obs_second(d):
            hop = 8 + jnp.where((d + a + zc) % 2 == 0, d, -d - 1)
            t = (zc + hop) % RING
            hs = t // 2
            wait_for(o1.at[hs], o1_r.at[hs])

            @pl.when(t != zc)
            def _():
                remote(o1.at[hs], o2.at[b], o2_s, o2_r.at[b], dev(h, t, q)).start()

            @pl.when(t == zc)
            def _():
                pltpu.make_async_copy(o1.at[hs], o2.at[b], o2_r.at[b]).start()

        loop(0, GROUPS, obs_second)
        kept = (zc % 2 == zc // 8).astype(jnp.int32)
        drains.append(lambda: wait_bytes(GROUPS - kept, o1.at[0], o2_s))

    def forward_x(it, c):
        pair(xb, u[it, c].reshape(3 * NZ, LANES))

        def forward(k):
            at = pl.ds(pl.multiple_of(k * 128, 128), 128)
            s1[it, c, pl.ds(k * 8, 8)] = times_pair(mh[at], ml[at], xb).reshape(8, 16, LANES)
            send_plane(s1.at[it, c], r1.at[it, c], a1_s.at[it, c], a1_r.at[it, c], k * 8, 8)

        loop(0, 4, forward)
        drains.append(lambda: wait_for(s1.at[it, c, pl.ds(0, PLANE - 1)], a1_s.at[it, c]))

    def forward_wait(it, c):
        wait_for(r1.at[it, c], a1_r.at[it, c])

    def forward_z(it, c):
        pair(zb, r1[it, c].reshape(ROWS, LANES))

        def blur_view(v):
            top, low = split(times_pair(nh[v], nl[v], zb))
            ztop[v, :, c * LANES : (c + 1) * LANES] = top
            zlow[v, :, c * LANES : (c + 1) * LANES] = low

        loop(0, Q, blur_view)

    def observed_third():
        start = (zc + jnp.where(zc % 2 == 1 - zc // 8, 0, 4)) % 8
        def obs_third(i):
            b = (start + jnp.where(i % 2 == 0, i // 2, -(i // 2) - 1) + 8) % 8
            wait_for(o2.at[b], o2_r.at[b])

            def one(i):
                mine = (b == h) & (i == q)
                dst = ob.at[q, pl.ds(h * 16, 16)]

                @pl.when(jnp.logical_not(mine))
                def _():
                    remote(o2.at[b, i], dst, o3_s, o3_r, dev(b, zc, i)).start()

                @pl.when(mine)
                def _():
                    pltpu.make_async_copy(o2.at[b, i], dst, o3_r).start()

            loop(0, Q, one)

        loop(0, GROUPS, obs_third)
        drains.append(lambda: wait_bytes(PLANE - 1, o1.at[0, 0], o3_s))

    def observed_wait():
        wait_for(ob, o3_r)

    def quotient():
        def view(v):
            blur = dot3(ztop[v], zlow[v], kyth[v], kytl[v])
            top, low = split(ob[v] / blur)
            top, low = split(dot3(top, low, kyh[v], kyl[v]))
            at = pl.ds(pl.multiple_of(v * NZ, NZ), NZ)
            for c in range(CHUNKS):
                wb[c, at, 0:LANES] = top[:, c * LANES : (c + 1) * LANES]
                wb[c, at, LANES:] = low[:, c * LANES : (c + 1) * LANES]

        loop(0, Q, view)

    def backward_z(it, c):
        def backward(k):
            at = pl.ds(pl.multiple_of(k * 128, 128), 128)
            s2[it, c, pl.ds(k * 8, 8)] = times_pair(nth[at], ntl[at], wb.at[c]).reshape(8, 16, LANES)
            send_plane(s2.at[it, c], r2.at[it, c], a2_s.at[it, c], a2_r.at[it, c], k * 8, 8)

        loop(0, 4, backward)
        drains.append(lambda: wait_for(s2.at[it, c, pl.ds(0, PLANE - 1)], a2_s.at[it, c]))

    def backward_wait(it, c):
        wait_for(r2.at[it, c], a2_r.at[it, c])

    def backward_x(it, c):
        pair(zb, r2[it, c].reshape(ROWS, LANES))

        def piece(k):
            return times_pair(mth[k * NZ : (k + 1) * NZ], mtl[k * NZ : (k + 1) * NZ], zb)

        back[it, c, 0] = piece(0)
        remote(back.at[it, c, 0], back.at[it, c, 4], bk_s.at[it, c, 0], bk_r.at[it, c, 0], dev(h, left, q)).start()
        back[it, c, 2] = piece(2)
        remote(back.at[it, c, 2], back.at[it, c, 3], bk_s.at[it, c, 1], bk_r.at[it, c, 1], dev(h, right, q)).start()
        back[it, c, 1] = piece(1)
        drains.append(lambda: [wait_for(back.at[it, c, 0], bk_s.at[it, c, k]) for k in range(2)])

    def back_wait(it, c):
        wait_for(back.at[it, c, 4], bk_r.at[it, c, 0])
        wait_for(back.at[it, c, 3], bk_r.at[it, c, 1])

    def update(it, c):
        u[it + 1, c, 1] = u[it, c, 1] * (back[it, c, 1] + back[it, c, 3] + back[it, c, 4]) * (1.0 / Q)

    def send_out(c):
        def one(i):
            j = (zc // 4 + i + 1) % J
            t = 4 * j + q
            src = u.at[ITERS, c, 1, pl.ds(j * 32, 32)]
            dst = out.at[0, pl.ds(zc * 32, 32), lanes(c)]

            @pl.when(t != zc)
            def _():
                remote(src, dst, uo_s.at[c], uo_r.at[c], dev(h, t, q)).start()

            @pl.when(t == zc)
            def _():
                pltpu.make_async_copy(src, dst, uo_r.at[c]).start()

        loop(0, J, one)
        kept = (zc % Q == q).astype(jnp.int32)
        drains.append(lambda: wait_bytes(J - kept, u.at[ITERS, c, 1, pl.ds(0, 32)], uo_s.at[c]))

    home = zc % Q
    role = q ^ home

    def pass_out(c):
        part = out.at[0, :, lanes(c)]

        @pl.when(role == 0)
        def _():
            wait_for(part, uo_r.at[c])
            remote(part, part, fw_s.at[c, 0], fa_r.at[c], dev(h, zc, q ^ 2)).start()
            remote(part, part, fw_s.at[c, 1], fb_r.at[c], dev(h, zc, q ^ 1)).start()

        @pl.when(role == 2)
        def _():
            wait_for(part, fa_r.at[c])
            remote(part, part, fw_s.at[c, 1], fb_r.at[c], dev(h, zc, q ^ 1)).start()

        def drain():
            @pl.when(role == 0)
            def _():
                wait_for(part, fw_s.at[c, 0])
                wait_for(part, fw_s.at[c, 1])

            @pl.when(role == 2)
            def _():
                wait_for(part, fw_s.at[c, 1])

            @pl.when((role == 1) | (role == 3))
            def _():
                wait_for(part, fb_r.at[c])

        drains.append(drain)

    phases = [(estimate_in,), (observed_first,), (taps_out,), (matrices,), (observed_second,)]
    for c in range(CHUNKS):
        phases += [(estimate_wait, c), (halo, 0, c)]
    for c in range(CHUNKS):
        phases += [(halo_wait, 0, c), (forward_x, 0, c)]
    for c in range(CHUNKS):
        phases += [(forward_wait, 0, c), (forward_z, 0, c)]
    phases += [(observed_third,), (observed_wait,)]
    for it in range(ITERS):
        phases.append((quotient,))
        steps = [[(backward_z, it)], [(backward_wait, it), (backward_x, it)]]
        if it + 1 < ITERS:
            steps += [
                [(back_wait, it), (update, it), (halo, it + 1)],
                [(halo_wait, it + 1), (forward_x, it + 1)],
                [(forward_wait, it + 1), (forward_z, it + 1)],
            ]
        else:
            steps += [[(back_wait, it), (update, it), (send_out,)], [(pass_out,)]]
        order = sorted((n - 1 + c if n else -1, n, c) for n in range(len(steps)) for c in range(CHUNKS))
        for _, n, c in order:
            phases += [(*phase, c) for phase in steps[n]]
    for phase, *args in phases:
        phase(*args)
    for done in drains:
        done()


def per_device(estimate, observed, psf_x, psf_y, psf_z):
    rows = jnp.concatenate([psf_x, psf_y, psf_z], axis=0)
    rows = jnp.concatenate([rows, jnp.flip(rows, axis=1)], axis=0)
    psf = jnp.pad(rows, ((0, 2), (0, 128 - TAPS)))
    recorded = jnp.transpose(observed[0], (1, 0, 2))
    vmem = pl.BlockSpec(memory_space=pltpu.VMEM)
    sem = pltpu.SemaphoreType.DMA
    return pl.pallas_call(
        kernel,
        out_shape=jax.ShapeDtypeStruct((1, 512, Y), F32),
        in_specs=[vmem] * 3,
        out_specs=vmem,
        scratch_shapes=[
            pltpu.VMEM((Q, 8, 128), F32),
            pltpu.VMEM((ROWS, Y), BF16),
            pltpu.VMEM((ROWS, Y), BF16),
            pltpu.VMEM((Y, ROWS), BF16),
            pltpu.VMEM((Y, ROWS), BF16),
            pltpu.VMEM((Q, NZ, ROWS), BF16),
            pltpu.VMEM((Q, NZ, ROWS), BF16),
            pltpu.VMEM((ROWS, Q * NZ), BF16),
            pltpu.VMEM((ROWS, Q * NZ), BF16),
            pltpu.VMEM((Q, Y, Y), BF16),
            pltpu.VMEM((Q, Y, Y), BF16),
            pltpu.VMEM((Q, Y, Y), BF16),
            pltpu.VMEM((Q, Y, Y), BF16),
            pltpu.VMEM((ITERS + 1, CHUNKS, 3, NZ, LANES), F32),
            pltpu.VMEM((ITERS, CHUNKS, PLANE, 16, LANES), F32),
            pltpu.VMEM((ITERS, CHUNKS, PLANE, 16, LANES), F32),
            pltpu.VMEM((ITERS, CHUNKS, PLANE, 16, LANES), F32),
            pltpu.VMEM((ITERS, CHUNKS, PLANE, 16, LANES), F32),
            pltpu.VMEM((ITERS, CHUNKS, 5, NZ, LANES), F32),
            pltpu.VMEM((3 * NZ, 2 * LANES), BF16),
            pltpu.VMEM((ROWS, 2 * LANES), BF16),
            pltpu.VMEM((Q, NZ, Y), BF16),
            pltpu.VMEM((Q, NZ, Y), BF16),
            pltpu.VMEM((CHUNKS, ROWS, 2 * LANES), BF16),
            pltpu.VMEM((GROUPS, 4, 16, Y), F32),
            pltpu.VMEM((GROUPS, 4, 16, Y), F32),
            pltpu.VMEM((Q, NZ, Y), F32),
            sem, sem,
            sem, sem((CHUNKS,)),
            sem((ITERS, CHUNKS, 2)), sem((ITERS, CHUNKS, 2)),
            sem((ITERS, CHUNKS)), sem((ITERS, CHUNKS)),
            sem((ITERS, CHUNKS)), sem((ITERS, CHUNKS)),
            sem((ITERS, CHUNKS, 2)), sem((ITERS, CHUNKS, 2)),
            sem, sem((GROUPS,)),
            sem, sem((GROUPS,)),
            sem, sem,
            sem((CHUNKS,)), sem((CHUNKS,)),
            sem((CHUNKS, 2)), sem((CHUNKS,)), sem((CHUNKS,)),
        ],
        compiler_params=pltpu.CompilerParams(
            collective_id=0, has_side_effects=True, vmem_limit_bytes=48 * 1024 * 1024
        ),
    )(estimate[0], recorded, psf)


def solution(mesh):
    return jax.shard_map(
        per_device,
        mesh=mesh,
        in_specs=(
            P("wide", None, None),
            P("view", None, "wide", None),
            P("view", None),
            P("view", None),
            P("view", None),
        ),
        out_specs=P("wide", None, None),
        check_vma=False,
    )
```

time: 550 us -> 183 us (0.33)
  the two profiles are of different devices: /device:TPU:1 before, /device:TPU:65 now
where the time goes in v2:
time: 183 us
  Pallas kernels  180 us (98%)
  local copies, waits for them, and re-layouts  3.02 us (2%)
    pallas_call x1, Pallas kernels, per_device(): pl.pallas_call(kernel, out_shape=jax.ShapeDtypeStruct((1, 512, Y), F32),...  180 us

profile of v2, /device:TPU:65, one launch (start us, length us, event | category | flops | bytes accessed | tf_op | source)
XLA Modules:
  0.0 182.7 jit_solution(16803129473847220864)
XLA Ops:
  0.0 0.0 copy-start.1
  0.0 0.0 copy-start.2
  0.0 0.0 copy-start.3
  0.0 0.6 copy-done.1
  0.7 0.0 copy-done.2
  0.7 0.0 copy-done.3
  0.7 0.1 rev.4
  0.8 0.0 copy-start
  0.8 1.3 copy.8
  2.1 0.1 copy-done
  2.2 179.7 %shard_map.55 = f32[1,512,384]{2,1,0:T(8,128)S(1)} custom-call(f32[512,384]{1,0:T(8,128)S(1)} %bitcast.7, f32[4,128,384]{2,1,0:T(8,128)S(1)} %bitcast.6, f32[8,128]{1,0:T(8,128)S(1)} %select_maximum_fusion.psf), custom_call_target="tpu_custom_call" | custom-call | tf_op jit(solution)/shard_map/pallas_call | solution.py:448
  181.9 0.9 copy.10
  (2 shorter events, 0.0 us)
Async XLA Ops:
  0.0 0.7 copy-start.1
  0.0 0.7 copy-start.2
  0.0 0.7 copy-start.3
  0.8 1.4 copy-start

commit v3 on v2

--- a/solution.py
+++ b/solution.py
@@ -23,6 +23,8 @@
 NZ = 128
 LANES = 128
 CHUNKS = Y // LANES
+FAR, NEAR = 0x2F5EB69A, 0x0C341D78
+SELF = PLANE - 2
 ROWS = PLANE * Q * J
 
 
@@ -53,18 +55,33 @@
 def kernel(
     est, obs, psf, out,
     taps, mh, ml, mth, mtl, nh, nl, nth, ntl, kyh, kyl, kyth, kytl,
-    u, s1, r1, s2, r2, back, xb, zb, ztop, zlow, wb, o1, o2, ob,
+    u, s1, r1, s2, r2, back, xb, zb, ztop, zlow, wb, o1, ob,
     psf_s, psf_r, uin_s, uin_r, halo_s, halo_r, a1_s, a1_r, a2_s, a2_r, bk_s, bk_r,
-    o1_s, o1_r, o2_s, o2_r, o3_s, o3_r, uo_s, uo_r, fw_s, fa_r, fb_r,
+    o1_s, o1_r, o3_s, o3_r, uo_s, uo_r, fw_s, fa_r, fb_r,
 ):
     q = lax.axis_index("view")
     w = lax.axis_index("wide")
-    h = w // RING
-    zc = w % RING
+    h = w >> 4
+    zc = w & 15
     p = h * Q + q
+    x_at, y_at = h & 3, (h >> 2) * 2 + (q >> 1)
 
     def dev(hh, zz, qq):
-        return {"view": qq, "wide": hh * RING + zz}
+        return {"view": qq, "wide": (hh << 4) | zz}
+
+    def offset(k):
+        step = k >> 1
+        code = (jnp.where(step < 8, FAR, NEAR) >> ((step & 7) * 4)) & 15
+        y = (y_at + (code >> 2)) & 3
+        return (x_at + (code & 3)) & 3, y, ((y & 1) << 1) | ((q ^ k) & 1)
+
+    def partner(k):
+        x, y, view = offset(k)
+        return ((y >> 1) << 4) | (x << 2) | view
+
+    def partner_dev(k):
+        x, y, view = offset(k)
+        return {"view": view, "wide": ((y >> 1) << 6) | (x << 4) | zc}
 
     def remote(src, dst, send, recv, where):
         return pltpu.make_async_remote_copy(
@@ -80,44 +97,46 @@
     barrier = pltpu.get_barrier_semaphore()
 
     def greet_ring(d):
-        pl.semaphore_signal(barrier, inc=1, device_id=dev(h, (zc + d) % RING, q), device_id_type=MESH)
+        pl.semaphore_signal(barrier, inc=1, device_id=dev(h, (zc + d) & 15, q), device_id_type=MESH)
 
     def greet_plane(d):
-        other = (p + d) % PLANE
-        pl.semaphore_signal(barrier, inc=1, device_id=dev(other // Q, zc, other % Q), device_id_type=MESH)
+        pl.semaphore_signal(barrier, inc=1, device_id=partner_dev(d), device_id_type=MESH)
 
     loop(1, RING, greet_ring)
-    loop(1, PLANE, greet_plane)
-    pl.semaphore_wait(barrier, RING - 1 + PLANE - 1)
+    loop(0, SELF, greet_plane)
+    greet_plane(SELF + 1)
+
+    from_self = (h == (zc & 7)) & ((zc & 1) == (zc >> 3))
+
+    def greet_source(i):
+        c, v = (h + (i >> 2)) & 7, (q + i) & 3
+
+        @pl.when(jnp.logical_not(from_self & (i == 0)))
+        def _():
+            pl.semaphore_signal(barrier, inc=1, device_id=dev(c, (zc & 1) * 8 + h, v), device_id_type=MESH)
+
+    loop(0, PLANE, greet_source)
+    pl.semaphore_wait(barrier, RING - 1 + PLANE - 1 + PLANE - from_self.astype(jnp.int32))
 
     def wait_bytes(count, ref, sem):
         loop(0, count, lambda i: wait_for(ref, sem))
 
     drains = []
-    owner = zc % Q == q
-    left = (zc + RING - 1) % RING
-    right = (zc + 1) % RING
-
-    def partner(k):
-        step = k // 2
-        x = (h + step) % 4
-        y = (h // 4 * 2 + q // 2 + step // 4 + step) % 4
-        return (y // 2 * 4 + x) * Q + y % 2 * 2 + (q + k) % 2
+    owner = (zc & 3) == q
+    left = (zc + RING - 1) & 15
+    right = (zc + 1) & 15
 
     def send_plane(send_buf, recv_buf, send, recv, first, count):
-        def one(i):
-            k = first + i
-            other = partner(k)
-
-            @pl.when(k != 0)
-            def _():
-                remote(send_buf.at[k], recv_buf.at[p], send, recv, dev(other // Q, zc, other % Q)).start()
-
-            @pl.when(k == 0)
-            def _():
-                pltpu.make_async_copy(send_buf.at[k], recv_buf.at[p], recv).start()
-
-        loop(0, count, one)
+        def one(k):
+            remote(send_buf.at[k], recv_buf.at[p], send, recv, partner_dev(k)).start()
+
+        last = first + count == PLANE
+        loop(first, first + count - jnp.where(last, 2, 0), one)
+
+        @pl.when(last)
+        def _():
+            pltpu.make_async_copy(send_buf.at[SELF], recv_buf.at[p], recv).start()
+            one(SELF + 1)
 
     def lanes(c):
         return pl.ds(c * LANES, LANES)
@@ -133,7 +152,7 @@
 
     def taps_out():
         def send_taps(d):
-            remote(psf, taps.at[q], psf_s, psf_r, dev(h, zc, (q + d) % Q)).start()
+            remote(psf, taps.at[q], psf_s, psf_r, dev(h, zc, (q + d) & 3)).start()
 
         loop(1, Q, send_taps)
         pltpu.make_async_copy(psf, taps.at[q], psf_r).start()
@@ -143,10 +162,10 @@
         @pl.when(owner)
         def _():
             for c in range(CHUNKS):
-                mine = u.at[0, c, 1, pl.ds((zc // 4) * 32, 32)]
+                mine = u.at[0, c, 1, pl.ds((zc >> 2) * 32, 32)]
 
                 def send(i):
-                    t = (zc + 8 + (1 - 2 * (i % 2)) * (i // 2)) % RING
+                    t = (zc + 8 + (1 - 2 * (i & 1)) * (i >> 1)) & 15
                     remote(est.at[pl.ds(t * 32, 32), lanes(c)], mine, uin_s, uin_r.at[c], dev(h, t, q)).start()
 
                 loop(1, RING, send)
@@ -164,7 +183,7 @@
 
     def observed_first():
         def obs_first(d):
-            c = (h + d) % GROUPS
+            c = (h + d) & 7
             remote(obs.at[:, pl.ds(c * 16, 16)], o1.at[h], o1_s, o1_r.at[h], dev(c, zc, q)).start()
 
         loop(1, GROUPS, obs_first)
@@ -191,37 +210,37 @@
         tt_mat = jnp.zeros((128, 128), F32)
         for v in range(Q):
             block = toeplitz(row_of(v, 0), 128, 128, 32 * v - 63)
-            tt_mat = jnp.where(k_lane // 32 == v, block, tt_mat)
+            tt_mat = jnp.where((k_lane >> 5) == v, block, tt_mat)
         tt_mat = jnp.where(((k_row >= 32) | low_ok) & ((k_row < 64) | high_ok), tt_mat, 0.0)
         t_top, t_low = split(t_mat)
         tt_top, tt_low = split(tt_mat)
         r_row, r_lane = iota((ROWS, 128), 0), iota((ROWS, 128), 1)
-        pick_rows = ((partner(r_row // 16) + 32 * ((r_row // 4) % 4)) == r_lane).astype(F32).astype(BF16)
+        pick_rows = ((partner(r_row >> 4) + 32 * ((r_row >> 2) & 3)) == r_lane).astype(F32).astype(BF16)
         c_row, c_lane = iota((128, Y), 0), iota((128, Y), 1)
-        pick_cols = ((c_lane // 128) * 32 + c_lane % 32 == c_row).astype(F32).astype(BF16)
-        same_j = (iota((ROWS, Y), 0) % 4) == ((iota((ROWS, Y), 1) // 32) % 4)
+        pick_cols = ((c_lane >> 7) * 32 + (c_lane & 31) == c_row).astype(F32).astype(BF16)
+        same_j = (iota((ROWS, Y), 0) & 3) == ((iota((ROWS, Y), 1) >> 5) & 3)
         for part, ref in ((t_top, mh), (t_low, ml)):
             rows = dot(pick_rows, part).astype(BF16)
             ref[...] = jnp.where(same_j, dot(rows, pick_cols), 0.0).astype(BF16)
         rt_row, rt_lane = iota((128, ROWS), 0), iota((128, ROWS), 1)
-        pick_rows_t = (((rt_lane // 16) + 32 * ((rt_lane // 4) % 4)) == rt_row).astype(F32).astype(BF16)
+        pick_rows_t = (((rt_lane >> 4) + 32 * ((rt_lane >> 2) & 3)) == rt_row).astype(F32).astype(BF16)
         ct_row, ct_lane = iota((Y, 128), 0), iota((Y, 128), 1)
-        pick_cols_t = ((ct_row // 128) * 32 + ct_row % 32 == ct_lane).astype(F32).astype(BF16)
-        same_j_t = (iota((Y, ROWS), 1) % 4) == ((iota((Y, ROWS), 0) // 32) % 4)
+        pick_cols_t = ((ct_row >> 7) * 32 + (ct_row & 31) == ct_lane).astype(F32).astype(BF16)
+        same_j_t = (iota((Y, ROWS), 1) & 3) == ((iota((Y, ROWS), 0) >> 5) & 3)
         for part, ref in ((tt_top, mth), (tt_low, mtl)):
             rows = dot(pick_cols_t, part).astype(BF16)
             ref[...] = jnp.where(same_j_t, dot(rows, pick_rows_t), 0.0).astype(BF16)
         g_row, g_lane = iota((128, ROWS), 0), iota((128, ROWS), 1)
-        g_pick = ((g_lane // 64) * 16 + (g_lane % 4) * 4 + (g_lane // 16) % 4) == g_row
+        g_pick = ((g_lane >> 6) * 16 + (g_lane & 3) * 4 + ((g_lane >> 4) & 3)) == g_row
         gt_row, gt_lane = iota((ROWS, 128), 0), iota((ROWS, 128), 1)
-        gt_p = partner(gt_row // 16)
-        gt_pick = ((gt_p // 4) * 16 + (gt_row % 4) * 4 + gt_p % 4) == gt_lane
+        gt_p = partner(gt_row >> 4)
+        gt_pick = ((gt_p >> 2) * 16 + (gt_row & 3) * 4 + (gt_p & 3)) == gt_lane
         for v in range(Q):
-            chosen = (g_pick & ((g_lane // 4) % 4 == v)).astype(F32).astype(BF16)
+            chosen = (g_pick & (((g_lane >> 2) & 3) == v)).astype(F32).astype(BF16)
             top, low = split(toeplitz(row_of(v, 5), NZ, NZ, -HALF))
             nh[v] = dot(top, chosen).astype(BF16)
             nl[v] = dot(low, chosen).astype(BF16)
-            chosen = (gt_pick & ((gt_row // 4) % 4 == v)).astype(F32).astype(BF16)
+            chosen = (gt_pick & (((gt_row >> 2) & 3) == v)).astype(F32).astype(BF16)
             top, low = split(toeplitz(row_of(v, 2), NZ, NZ, -HALF))
             nth[:, v * NZ : (v + 1) * NZ] = dot(chosen, top).astype(BF16)
             ntl[:, v * NZ : (v + 1) * NZ] = dot(chosen, low).astype(BF16)
@@ -243,26 +262,32 @@
         wait_for(u.at[it, c, 0], halo_r.at[it, c, 1])
 
     def observed_second():
-        a = zc // 8
-        b = zc % 8
+        a = zc >> 3
+        b = zc & 7
+        dst = ob.at[q, pl.ds(h * 16, 16)]
 
         def obs_second(d):
-            hop = 8 + jnp.where((d + a + zc) % 2 == 0, d, -d - 1)
-            t = (zc + hop) % RING
-            hs = t // 2
+            hop = 8 + jnp.where(((d + a + zc) & 1) == 0, d, -d - 1)
+            t = (zc + hop) & 15
+            hs = t >> 1
             wait_for(o1.at[hs], o1_r.at[hs])
 
-            @pl.when(t != zc)
-            def _():
-                remote(o1.at[hs], o2.at[b], o2_s, o2_r.at[b], dev(h, t, q)).start()
-
-            @pl.when(t == zc)
-            def _():
-                pltpu.make_async_copy(o1.at[hs], o2.at[b], o2_r.at[b]).start()
+            def one(k):
+                i = (q + k) & 3
+                mine = (b == h) & (t == zc) & (k == 0)
+
+                @pl.when(jnp.logical_not(mine))
+                def _():
+                    remote(o1.at[hs, i], dst, o3_s, o3_r, dev(b, t, i)).start()
+
+                @pl.when(mine)
+                def _():
+                    pltpu.make_async_copy(o1.at[hs, i], dst, o3_r).start()
+
+            loop(0, Q, one)
 
         loop(0, GROUPS, obs_second)
-        kept = (zc % 2 == zc // 8).astype(jnp.int32)
-        drains.append(lambda: wait_bytes(GROUPS - kept, o1.at[0], o2_s))
+        drains.append(lambda: wait_bytes(PLANE - from_self.astype(jnp.int32), o1.at[0, 0], o3_s))
 
     def forward_x(it, c):
         pair(xb, u[it, c].reshape(3 * NZ, LANES))
@@ -287,29 +312,6 @@
             zlow[v, :, c * LANES : (c + 1) * LANES] = low
 
         loop(0, Q, blur_view)
-
-    def observed_third():
-        start = (zc + jnp.where(zc % 2 == 1 - zc // 8, 0, 4)) % 8
-        def obs_third(i):
-            b = (start + jnp.where(i % 2 == 0, i // 2, -(i // 2) - 1) + 8) % 8
-            wait_for(o2.at[b], o2_r.at[b])
-
-            def one(i):
-                mine = (b == h) & (i == q)
-                dst = ob.at[q, pl.ds(h * 16, 16)]
-
-                @pl.when(jnp.logical_not(mine))
-                def _():
-                    remote(o2.at[b, i], dst, o3_s, o3_r, dev(b, zc, i)).start()
-
-                @pl.when(mine)
-                def _():
-                    pltpu.make_async_copy(o2.at[b, i], dst, o3_r).start()
-
-            loop(0, Q, one)
-
-        loop(0, GROUPS, obs_third)
-        drains.append(lambda: wait_bytes(PLANE - 1, o1.at[0, 0], o3_s))
 
     def observed_wait():
         wait_for(ob, o3_r)
@@ -360,7 +362,7 @@
 
     def send_out(c):
         def one(i):
-            j = (zc // 4 + i + 1) % J
+            j = ((zc >> 2) + i + 1) & 3
             t = 4 * j + q
             src = u.at[ITERS, c, 1, pl.ds(j * 32, 32)]
             dst = out.at[0, pl.ds(zc * 32, 32), lanes(c)]
@@ -374,10 +376,10 @@
                 pltpu.make_async_copy(src, dst, uo_r.at[c]).start()
 
         loop(0, J, one)
-        kept = (zc % Q == q).astype(jnp.int32)
+        kept = ((zc & 3) == q).astype(jnp.int32)
         drains.append(lambda: wait_bytes(J - kept, u.at[ITERS, c, 1, pl.ds(0, 32)], uo_s.at[c]))
 
-    home = zc % Q
+    home = zc & 3
     role = q ^ home
 
     def pass_out(c):
@@ -410,14 +412,15 @@
 
         drains.append(drain)
 
-    phases = [(estimate_in,), (observed_first,), (taps_out,), (matrices,), (observed_second,)]
+    phases = [(estimate_in,), (observed_first,), (taps_out,), (matrices,)]
     for c in range(CHUNKS):
         phases += [(estimate_wait, c), (halo, 0, c)]
+    phases.append((observed_second,))
     for c in range(CHUNKS):
         phases += [(halo_wait, 0, c), (forward_x, 0, c)]
     for c in range(CHUNKS):
         phases += [(forward_wait, 0, c), (forward_z, 0, c)]
-    phases += [(observed_third,), (observed_wait,)]
+    phases.append((observed_wait,))
     for it in range(ITERS):
         phases.append((quotient,))
         steps = [[(backward_z, it)], [(backward_wait, it), (backward_x, it)]]
@@ -476,7 +479,6 @@
             pltpu.VMEM((Q, NZ, Y), BF16),
             pltpu.VMEM((CHUNKS, ROWS, 2 * LANES), BF16),
             pltpu.VMEM((GROUPS, 4, 16, Y), F32),
-            pltpu.VMEM((GROUPS, 4, 16, Y), F32),
             pltpu.VMEM((Q, NZ, Y), F32),
             sem, sem,
             sem, sem((CHUNKS,)),
@@ -484,7 +486,6 @@
             sem((ITERS, CHUNKS)), sem((ITERS, CHUNKS)),
             sem((ITERS, CHUNKS)), sem((ITERS, CHUNKS)),
             sem((ITERS, CHUNKS, 2)), sem((ITERS, CHUNKS, 2)),
-            sem, sem((GROUPS,)),
             sem, sem((GROUPS,)),
             sem, sem,
             sem((CHUNKS,)), sem((CHUNKS,)),

time: 183 us -> 164 us (0.90)
  the two profiles are of different devices: /device:TPU:65 before, /device:TPU:15 now
where the time goes in v3:
time: 164 us
  Pallas kernels  161 us (98%)
  local copies, waits for them, and re-layouts  3.02 us (2%)
    pallas_call x1, Pallas kernels, per_device(): pl.pallas_call(kernel, out_shape=jax.ShapeDtypeStruct((1, 512, Y), F32),...  161 us

profile of v3, /device:TPU:15, one launch (start us, length us, event | category | flops | bytes accessed | tf_op | source)
XLA Modules:
  0.0 164.0 jit_solution(7954414435459480826)
XLA Ops:
  0.0 0.0 copy-start.1
  0.0 0.0 copy-start.2
  0.0 0.0 copy-start.3
  0.0 0.6 copy-done.1
  0.7 0.0 copy-done.2
  0.7 0.0 copy-done.3
  0.7 0.1 rev.4
  0.8 0.0 copy-start
  0.8 1.3 copy.8
  2.1 0.1 copy-done
  2.2 161.0 %shard_map.55 = f32[1,512,384]{2,1,0:T(8,128)S(1)} custom-call(f32[512,384]{1,0:T(8,128)S(1)} %bitcast.7, f32[4,128,384]{2,1,0:T(8,128)S(1)} %bitcast.6, f32[8,128]{1,0:T(8,128)S(1)} %select_maximum_fusion.psf), custom_call_target="tpu_custom_call" | custom-call | tf_op jit(solution)/shard_map/pallas_call | solution.py:451
  163.1 0.9 copy.10
  (2 shorter events, 0.0 us)
Async XLA Ops:
  0.0 0.7 copy-start.1
  0.0 0.7 copy-start.2
  0.0 0.7 copy-start.3
  0.8 1.4 copy-start

commit v4 on v3

--- a/solution.py
+++ b/solution.py
@@ -55,7 +55,7 @@
 def kernel(
     est, obs, psf, out,
     taps, mh, ml, mth, mtl, nh, nl, nth, ntl, kyh, kyl, kyth, kytl,
-    u, s1, r1, s2, r2, back, xb, zb, ztop, zlow, wb, o1, ob,
+    u, s1, r1, s2, r2, back, xb, zb, ztop, zlow, wb, blur, o1, ob,
     psf_s, psf_r, uin_s, uin_r, halo_s, halo_r, a1_s, a1_r, a2_s, a2_r, bk_s, bk_r,
     o1_s, o1_r, o3_s, o3_r, uo_s, uo_r, fw_s, fa_r, fb_r,
 ):
@@ -126,17 +126,13 @@
     left = (zc + RING - 1) & 15
     right = (zc + 1) & 15
 
-    def send_plane(send_buf, recv_buf, send, recv, first, count):
+    def send_plane(send_buf, recv_buf, send, recv):
         def one(k):
             remote(send_buf.at[k], recv_buf.at[p], send, recv, partner_dev(k)).start()
 
-        last = first + count == PLANE
-        loop(first, first + count - jnp.where(last, 2, 0), one)
-
-        @pl.when(last)
-        def _():
-            pltpu.make_async_copy(send_buf.at[SELF], recv_buf.at[p], recv).start()
-            one(SELF + 1)
+        loop(0, SELF, one)
+        one(SELF + 1)
+        pltpu.make_async_copy(send_buf.at[SELF], recv_buf.at[p], recv).start()
 
     def lanes(c):
         return pl.ds(c * LANES, LANES)
@@ -292,12 +288,8 @@
     def forward_x(it, c):
         pair(xb, u[it, c].reshape(3 * NZ, LANES))
 
-        def forward(k):
-            at = pl.ds(pl.multiple_of(k * 128, 128), 128)
-            s1[it, c, pl.ds(k * 8, 8)] = times_pair(mh[at], ml[at], xb).reshape(8, 16, LANES)
-            send_plane(s1.at[it, c], r1.at[it, c], a1_s.at[it, c], a1_r.at[it, c], k * 8, 8)
-
-        loop(0, 4, forward)
+        s1[it, c] = times_pair(mh[...], ml[...], xb).reshape(PLANE, 16, LANES)
+        send_plane(s1.at[it, c], r1.at[it, c], a1_s.at[it, c], a1_r.at[it, c])
         drains.append(lambda: wait_for(s1.at[it, c, pl.ds(0, PLANE - 1)], a1_s.at[it, c]))
 
     def forward_wait(it, c):
@@ -306,20 +298,23 @@
     def forward_z(it, c):
         pair(zb, r1[it, c].reshape(ROWS, LANES))
 
-        def blur_view(v):
-            top, low = split(times_pair(nh[v], nl[v], zb))
-            ztop[v, :, c * LANES : (c + 1) * LANES] = top
-            zlow[v, :, c * LANES : (c + 1) * LANES] = low
-
-        loop(0, Q, blur_view)
+        rows = Q * NZ
+        top, low = split(times_pair(nh[...].reshape(rows, ROWS), nl[...].reshape(rows, ROWS), zb))
+        ztop[:, :, c * LANES : (c + 1) * LANES] = top.reshape(Q, NZ, LANES)
+        zlow[:, :, c * LANES : (c + 1) * LANES] = low.reshape(Q, NZ, LANES)
 
     def observed_wait():
         wait_for(ob, o3_r)
 
+    def forward_y():
+        def view(v):
+            blur[v] = dot3(ztop[v], zlow[v], kyth[v], kytl[v])
+
+        loop(0, Q, view)
+
     def quotient():
         def view(v):
-            blur = dot3(ztop[v], zlow[v], kyth[v], kytl[v])
-            top, low = split(ob[v] / blur)
+            top, low = split(ob[v] / blur[v])
             top, low = split(dot3(top, low, kyh[v], kyl[v]))
             at = pl.ds(pl.multiple_of(v * NZ, NZ), NZ)
             for c in range(CHUNKS):
@@ -329,12 +324,8 @@
         loop(0, Q, view)
 
     def backward_z(it, c):
-        def backward(k):
-            at = pl.ds(pl.multiple_of(k * 128, 128), 128)
-            s2[it, c, pl.ds(k * 8, 8)] = times_pair(nth[at], ntl[at], wb.at[c]).reshape(8, 16, LANES)
-            send_plane(s2.at[it, c], r2.at[it, c], a2_s.at[it, c], a2_r.at[it, c], k * 8, 8)
-
-        loop(0, 4, backward)
+        s2[it, c] = times_pair(nth[...], ntl[...], wb.at[c]).reshape(PLANE, 16, LANES)
+        send_plane(s2.at[it, c], r2.at[it, c], a2_s.at[it, c], a2_r.at[it, c])
         drains.append(lambda: wait_for(s2.at[it, c, pl.ds(0, PLANE - 1)], a2_s.at[it, c]))
 
     def backward_wait(it, c):
@@ -412,7 +403,7 @@
 
         drains.append(drain)
 
-    phases = [(estimate_in,), (observed_first,), (taps_out,), (matrices,)]
+    phases = [(taps_out,), (observed_first,), (estimate_in,), (matrices,)]
     for c in range(CHUNKS):
         phases += [(estimate_wait, c), (halo, 0, c)]
     phases.append((observed_second,))
@@ -420,9 +411,9 @@
         phases += [(halo_wait, 0, c), (forward_x, 0, c)]
     for c in range(CHUNKS):
         phases += [(forward_wait, 0, c), (forward_z, 0, c)]
-    phases.append((observed_wait,))
+    phases += [(forward_y,), (observed_wait,)]
     for it in range(ITERS):
-        phases.append((quotient,))
+        phases += [(quotient,)] if it == 0 else [(forward_y,), (quotient,)]
         steps = [[(backward_z, it)], [(backward_wait, it), (backward_x, it)]]
         if it + 1 < ITERS:
             steps += [
@@ -432,7 +423,8 @@
             ]
         else:
             steps += [[(back_wait, it), (update, it), (send_out,)], [(pass_out,)]]
-        order = sorted((n - 1 + c if n else -1, n, c) for n in range(len(steps)) for c in range(CHUNKS))
+        last = len(steps) - 1
+        order = sorted((99 if n == last else n - 1 + c if n else -1, n, c) for n in range(last + 1) for c in range(CHUNKS))
         for _, n, c in order:
             phases += [(*phase, c) for phase in steps[n]]
     for phase, *args in phases:
@@ -478,6 +470,7 @@
             pltpu.VMEM((Q, NZ, Y), BF16),
             pltpu.VMEM((Q, NZ, Y), BF16),
             pltpu.VMEM((CHUNKS, ROWS, 2 * LANES), BF16),
+            pltpu.VMEM((Q, NZ, Y), F32),
             pltpu.VMEM((GROUPS, 4, 16, Y), F32),
             pltpu.VMEM((Q, NZ, Y), F32),
             sem, sem,

time: 164 us -> 157 us (0.957)
  the two profiles are of different devices: /device:TPU:15 before, /device:TPU:9 now
where the time goes in v4:
time: 157 us
  Pallas kernels  154 us (98%)
  local copies, waits for them, and re-layouts  3.02 us (2%)
    pallas_call x1, Pallas kernels, per_device(): pl.pallas_call(kernel, out_shape=jax.ShapeDtypeStruct((1, 512, Y), F32),...  154 us

profile of v4, /device:TPU:9, one launch (start us, length us, event | category | flops | bytes accessed | tf_op | source)
XLA Modules:
  0.0 157.1 jit_solution(17616386740397893164)
XLA Ops:
  0.0 0.0 copy-start.1
  0.0 0.0 copy-start.2
  0.0 0.0 copy-start.3
  0.0 0.6 copy-done.1
  0.7 0.0 copy-done.2
  0.7 0.0 copy-done.3
  0.7 0.1 rev.4
  0.8 0.0 copy-start
  0.8 1.3 copy.8
  2.1 0.1 copy-done
  2.2 154.0 %shard_map.55 = f32[1,512,384]{2,1,0:T(8,128)S(1)} custom-call(f32[512,384]{1,0:T(8,128)S(1)} %bitcast.7, f32[4,128,384]{2,1,0:T(8,128)S(1)} %bitcast.6, f32[8,128]{1,0:T(8,128)S(1)} %select_maximum_fusion.psf), custom_call_target="tpu_custom_call" | custom-call | tf_op jit(solution)/shard_map/pallas_call | solution.py:443
  156.2 0.9 copy.10
  (2 shorter events, 0.0 us)
Async XLA Ops:
  0.0 0.7 copy-start.1
  0.0 0.7 copy-start.2
  0.0 0.7 copy-start.3
  0.8 1.4 copy-start

commit v5 on v4

--- a/solution.py
+++ b/solution.py
@@ -360,11 +360,11 @@
 
             @pl.when(t != zc)
             def _():
-                remote(src, dst, uo_s.at[c], uo_r.at[c], dev(h, t, q)).start()
+                remote(src, dst, uo_s.at[c], uo_r.at[c, zc >> 3], dev(h, t, q)).start()
 
             @pl.when(t == zc)
             def _():
-                pltpu.make_async_copy(src, dst, uo_r.at[c]).start()
+                pltpu.make_async_copy(src, dst, uo_r.at[c, zc >> 3]).start()
 
         loop(0, J, one)
         kept = ((zc & 3) == q).astype(jnp.int32)
@@ -375,17 +375,20 @@
 
     def pass_out(c):
         part = out.at[0, :, lanes(c)]
+        halves = [out.at[0, pl.ds(k * 256, 256), lanes(c)] for k in range(2)]
 
         @pl.when(role == 0)
         def _():
-            wait_for(part, uo_r.at[c])
-            remote(part, part, fw_s.at[c, 0], fa_r.at[c], dev(h, zc, q ^ 2)).start()
-            remote(part, part, fw_s.at[c, 1], fb_r.at[c], dev(h, zc, q ^ 1)).start()
+            for k, half in enumerate(halves):
+                wait_for(half, uo_r.at[c, k])
+                remote(half, half, fw_s.at[c, 0], fa_r.at[c, k], dev(h, zc, q ^ 2)).start()
+                remote(half, half, fw_s.at[c, 1], fb_r.at[c, k], dev(h, zc, q ^ 1)).start()
 
         @pl.when(role == 2)
         def _():
-            wait_for(part, fa_r.at[c])
-            remote(part, part, fw_s.at[c, 1], fb_r.at[c], dev(h, zc, q ^ 1)).start()
+            for k, half in enumerate(halves):
+                wait_for(half, fa_r.at[c, k])
+                remote(half, half, fw_s.at[c, 1], fb_r.at[c, k], dev(h, zc, q ^ 1)).start()
 
         def drain():
             @pl.when(role == 0)
@@ -399,7 +402,8 @@
 
             @pl.when((role == 1) | (role == 3))
             def _():
-                wait_for(part, fb_r.at[c])
+                for k, half in enumerate(halves):
+                    wait_for(half, fb_r.at[c, k])
 
         drains.append(drain)
 
@@ -481,8 +485,8 @@
             sem((ITERS, CHUNKS, 2)), sem((ITERS, CHUNKS, 2)),
             sem, sem((GROUPS,)),
             sem, sem,
-            sem((CHUNKS,)), sem((CHUNKS,)),
-            sem((CHUNKS, 2)), sem((CHUNKS,)), sem((CHUNKS,)),
+            sem((CHUNKS,)), sem((CHUNKS, 2)),
+            sem((CHUNKS, 2)), sem((CHUNKS, 2)), sem((CHUNKS, 2)),
         ],
         compiler_params=pltpu.CompilerParams(
             collective_id=0, has_side_effects=True, vmem_limit_bytes=48 * 1024 * 1024

time: 157 us -> 156 us (level)
  no operation moved by 1% of the time
where the time goes in v5:
time: 156 us
  Pallas kernels  153 us (98%)
  local copies, waits for them, and re-layouts  3.02 us (2%)
    pallas_call x1, Pallas kernels, per_device(): pl.pallas_call(kernel, out_shape=jax.ShapeDtypeStruct((1, 512, Y), F32),...  153 us

profile of v5, /device:TPU:9, one launch (start us, length us, event | category | flops | bytes accessed | tf_op | source)
XLA Modules:
  0.0 155.6 jit_solution(1186190258696499945)
XLA Ops:
  0.0 0.0 copy-start.1
  0.0 0.0 copy-start.2
  0.0 0.0 copy-start.3
  0.0 0.6 copy-done.1
  0.7 0.0 copy-done.2
  0.7 0.0 copy-done.3
  0.7 0.1 rev.4
  0.8 0.0 copy-start
  0.8 1.3 copy.8
  2.1 0.1 copy-done
  2.2 152.5 %shard_map.55 = f32[1,512,384]{2,1,0:T(8,128)S(1)} custom-call(f32[512,384]{1,0:T(8,128)S(1)} %bitcast.7, f32[4,128,384]{2,1,0:T(8,128)S(1)} %bitcast.6, f32[8,128]{1,0:T(8,128)S(1)} %select_maximum_fusion.psf), custom_call_target="tpu_custom_call" | custom-call | tf_op jit(solution)/shard_map/pallas_call | solution.py:447
  154.7 0.9 copy.10
  (2 shorter events, 0.0 us)
Async XLA Ops:
  0.0 0.7 copy-start.1
  0.0 0.7 copy-start.2
  0.0 0.7 copy-start.3
  0.8 1.4 copy-start
